TPU v7x, 256 devices: a whole 4x4x8 slice. The times are simulated.
256 devices in a mesh: seq: 32 (over z, y), head: 8 (over x, core).
Axes of the slice: x: 4, y: 4, z: 8, core: 2. Of those that a mesh axis runs over, the one named last changes fastest.
Arguments:
- queries: bfloat16 [16384, 4096], P('seq', 'head'), may hold values from -6 to 6
- keys: bfloat16 [16384, 4096], P('seq', 'head'), may hold values from -6 to 6
- values: bfloat16 [16384, 4096], P('seq', 'head'), may hold values from -6 to 6
- gate: bfloat16 [16384, 4096], P('seq', 'head'), may hold values from -6 to 6
- log_decay: bfloat16 [16, 16384], P('head', 'seq'), may hold values from -3 to 0
- trunc_blocks: int32 [16], P('head'), may hold values from 2 to 64, as said below
- norm_gain: bfloat16 [4096], P('head'), may hold values from 0.099609375 to 1.8984375
- w_out: bfloat16 [4096, 4096], P('head'), may hold values from -0.09375 to 0.09375
Outputs:
- mixed: bfloat16 [16384, 4096], P(('seq', 'head'))
Inputs may be any that keep to these rules, and one draw needn't show every extreme that they name: `trunc_blocks`: each head's value is 2 or 64, and both values occur.
All inputs are finite; a program needn't handle non-finite values.
Results may differ from a plain program's by a relative error of at most 0.02.
Values may be sent and summed in bfloat16 or wider, within the bound.
A program may use at most 64 MiB of HBM per device.

v0:
```python
import math

import jax
import jax.numpy as jnp
from jax import lax
from jax.sharding import PartitionSpec as P

BLOCK = 256
FAST = 2


def from_behind(value, axis, steps):
    count = lax.axis_size(axis)
    initial, last = (max(0, -steps), min(count, count - steps))
    return lax.ppermute(value, axis, [(source, source + steps) for source in range(initial, last)])


def on_device(queries, keys, values, gate, log_decay, trunc_blocks, norm_gain, w_out):
    tok_rows = queries.shape[0]
    head_count = trunc_blocks.shape[0]
    head_size = queries.shape[1] // head_count
    seq_count = lax.axis_size("seq")
    block_total = tok_rows // BLOCK * seq_count
    query_heads = queries.reshape(tok_rows, head_count, head_size)
    key_heads = keys.reshape(tok_rows, head_count, head_size)
    value_heads = values.reshape(tok_rows, head_count, head_size)
    cumulative = jnp.cumsum(log_decay.astype(jnp.float32), axis=1)
    segment_log = cumulative[:, -1]
    is_fast = trunc_blocks < block_total
    reach = jnp.where(is_fast, trunc_blocks, block_total)
    slow_mask = jnp.where(is_fast, 0.0, 1.0).astype(jnp.float32)
    key_index = jnp.arange(tok_rows)
    block_rows = math.gcd(tok_rows, 512)
    scores = jnp.einsum("thd,shd->hts", query_heads, key_heads, preferred_element_type=jnp.float32)
    decay = jnp.exp(jnp.minimum(cumulative[:, :, None] - cumulative[:, None, :], 0.0))
    query_index = 0 + jnp.arange(block_rows)
    causal = key_index[None, :] <= query_index[:, None]
    block_gap = query_index[:, None] // BLOCK - key_index[None, :] // BLOCK
    visible = causal[None] & (block_gap[None] <= reach[:, None, None])
    weights = jnp.where(visible, scores * decay, 0.0).astype(jnp.bfloat16)
    pieces = jnp.einsum("hts,shd->thd", weights, value_heads, preferred_element_type=jnp.float32)
    window = pieces
    edge_rows = FAST * BLOCK
    tail_keys, tail_values, tail_rates = from_behind((keys, values, log_decay), "seq", 1)
    tail_logs = tail_rates.astype(jnp.float32)
    suffix = jnp.sum(tail_logs, axis=1, keepdims=True) - jnp.cumsum(tail_logs, axis=1)
    edge_scores = jnp.einsum(
        "thd,shd->hts",
        query_heads,
        tail_keys.reshape(edge_rows, head_count, head_size),
        preferred_element_type=jnp.float32,
    )
    edge_decay = jnp.exp(cumulative[:, :, None] + suffix[:, None, :])
    edge_index = jnp.arange(edge_rows)
    edge_gap = edge_index[:, None] // BLOCK - (edge_index[None, :] // BLOCK - FAST)
    edge_mask = (edge_gap[None] <= reach[:, None, None]) & is_fast[:, None, None]
    edge_weights = jnp.where(edge_mask, edge_scores * edge_decay, 0.0).astype(jnp.bfloat16)
    remote = jnp.einsum(
        "hts,shd->thd",
        edge_weights,
        tail_values.reshape(edge_rows, head_count, head_size),
        preferred_element_type=jnp.float32,
    )
    window = jnp.concatenate([window + remote, window[edge_rows:]], 0)
    decayed = (
        key_heads.astype(jnp.float32) * jnp.exp(segment_log[:, None] - cumulative).T[:, :, None]
    )
    local_state = jnp.einsum(
        "shd,she->hde", decayed, value_heads.astype(jnp.float32), precision=lax.Precision.HIGHEST
    )
    totals, states = (
        lax.all_gather(segment_log[None].astype(jnp.bfloat16), "seq", axis=0, tiled=True).astype(
            jnp.float32
        ),
        lax.all_gather(local_state[None].astype(jnp.bfloat16), "seq", axis=0, tiled=True).astype(
            jnp.float32
        ),
    )
    position = lax.axis_index("seq")
    end_logs = jnp.cumsum(totals, axis=0)
    start_log = lax.dynamic_index_in_dim(end_logs, position, 0, False) - lax.dynamic_index_in_dim(
        totals, position, 0, False
    )
    earlier = (jnp.arange(seq_count) < position)[:, None]
    factor = jnp.where(
        earlier, jnp.exp(jnp.where(earlier, start_log[None, :] - end_logs, 0.0)), 0.0
    )
    prior_state = jnp.einsum("nh,nhde->hde", factor, states, precision=lax.Precision.HIGHEST)
    carried = jnp.einsum(
        "thd,hde->the",
        query_heads.astype(jnp.float32),
        prior_state,
        precision=lax.Precision.HIGHEST,
    )
    carried = carried * (jnp.exp(cumulative) * slow_mask[:, None]).T[:, :, None]
    retained = window + carried
    row_mean = jnp.mean(retained, axis=-1, keepdims=True)
    centered = retained - row_mean
    row_var = jnp.mean(centered * centered, axis=-1, keepdims=True)
    normed = (centered * lax.rsqrt(row_var + 1e-05)).reshape(tok_rows, head_count * head_size)
    hidden = (
        normed * norm_gain.astype(jnp.float32) * jax.nn.silu(gate.astype(jnp.float32))
    ).astype(jnp.bfloat16)
    mixed = lax.psum_scatter(
        jnp.dot(hidden, w_out, preferred_element_type=jnp.float32).astype(jnp.bfloat16),
        "head",
        scatter_dimension=0,
        tiled=True,
    )
    return mixed


def solution(mesh):
    in_specs = (
        P("seq", "head"),
        P("seq", "head"),
        P("seq", "head"),
        P("seq", "head"),
        P("head", "seq"),
        P("head"),
        P("head"),
        P("head", None),
    )
    out_specs = P(("seq", "head"), None)
    return jax.shard_map(
        on_device, mesh=mesh, in_specs=in_specs, out_specs=out_specs, check_vma=False
    )
```

profile of v0, /device:TPU:8, one launch (start us, length us, event | category | flops | bytes accessed | tf_op | source)
XLA Modules:
  0.0 191.8 jit_solution(13593956683482940884)
XLA Ops:
  6.5 0.8 reshape.273
  7.3 0.6 reduce-window.14
  8.1 0.2 reduce-window.15
  8.5 0.7 broadcast_select_fusion
  9.2 1.3 copy.56
  10.5 2.4 %convolution_convert_fusion.1 = bf16[2,256,256]{2,1,0:T(8,128)(2,1)} fusion(bf16[512,2,256]{0,2,1:T(8,128)(2,1)S(1)} %bitcast.67, f32[512,2]{0,1:T(2,128)S(1)} %get-tuple-element.6, bf16[64,2,8,256]{3,2,1,0:T(8,128)(2,1)} %bitcast.18), kind=kOutput, calls=%fused_computation.12 | convolution fusion | flops 805961728 | bytes 1314816 | tf_op jit(solution)/shard_map/shd,she->hde/dot_general | solution.py:68
  13.0 3.5 %collective-permute-start.1 = (bf16[2,512]{1,0:T(2,128)(2,1)S(1)}, bf16[2,512]{1,0:T(2,128)(2,1)S(1)}, u32[]{:S(2)}, u32[]{:S(2)}) collective-permute-start(bf16[2,512]{1,0:T(2,128)(2,1)S(1)} %copy-done.1), channel_id=1, source_target_pairs={{0,8},{8,16},{16,24},{24,32},{32,40},{40,48},{48,56},{56,64},{64,7... | collective-permute-start | bytes 6152 | tf_op jit(solution)/shard_map/ppermute | solution.py:15
  16.5 3.2 %collective-permute-start = (bf16[512,512]{0,1:T(8,128)(2,1)S(1)}, bf16[512,512]{0,1:T(8,128)(2,1)}, u32[]{:S(2)}, u32[]{:S(2)}) collective-permute-start(bf16[512,512]{0,1:T(8,128)(2,1)S(1)} %copy.56), channel_id=1, source_target_pairs={{0,8},{8,16},{16,24},{24,32},{32,40},{40,48},{48,56},{56,64},{64,7... | collective-permute-start | bytes 1572872 | tf_op jit(solution)/shard_map/ppermute | solution.py:15
  19.7 3.5 %collective-permute-start.2 = (bf16[512,512]{1,0:T(8,128)(2,1)}, bf16[512,512]{1,0:T(8,128)(2,1)S(1)}, u32[]{:S(2)}, u32[]{:S(2)}) collective-permute-start(bf16[512,512]{1,0:T(8,128)(2,1)} %param.10), channel_id=1, source_target_pairs={{0,8},{8,16},{16,24},{24,32},{32,40},{40,48},{48,56},{56,64},{64,7... | collective-permute-start | bytes 1572872 | tf_op jit(solution)/shard_map/ppermute | solution.py:15
  23.2 0.6 dynamic-slice
  24.5 0.2 dynamic-update-slice
  24.7 91.9 %all-reduce = bf16[64]{0:T(256)(128)(2,1)S(1)} all-reduce(bf16[64]{0:T(256)(128)(2,1)S(1)} %dynamic-update-slice), channel_id=2, replica_groups=mesh['seq'=32,'head'=8] {'seq'}, use_global_device_ids=true, to_apply=%add | all-reduce | flops 64 | bytes 256
  117.0 0.2 broadcast_subtract_fusion
  117.2 3.5 %fusion.3 = f32[2,512,256]{1,2,0:T(8,128)} fusion(bf16[512,2,256]{0,2,1:T(8,128)(2,1)S(1)} %bitcast.68, f32[2,512]{1,0:T(2,128)S(1)} %bitcast.74, s32[512,512]{1,0:T(8,128)S(1)} %get-tuple-element.8, s32[2]{0:T(128)S(1)} %broadcast_select_fusion.1, pred[512,512]{1,0:T(8,128)(4,1)S(1)} %iota_compare_fusion, bf16[64,2,8,256]{3,2,1,0:T(8,128)(2,1)} %bitcast.18, ...), kind=kOutput, calls=%fused_computation.11 | convolution fusion | flops 540540928 | bytes 3936264 | tf_op jit(solution)/shard_map/hts,shd->thd/dot_general | solution.py:41
  120.8 0.6 reduce-window.16
  121.6 0.2 reduce-window.19
  122.0 1.0 copy.39
  123.0 2.8 %fusion.2 = f32[512,2,256]{0,2,1:T(8,128)S(1)} fusion(f32[2,512,256]{1,2,0:T(8,128)} %fusion.3, bf16[512,2,256]{0,2,1:T(8,128)(2,1)} %bitcast.69, bf16[512,2,256]{0,2,1:T(8,128)(2,1)} %bitcast.2, f32[2,512]{1,0:T(2,128)S(1)} %bitcast_subtract_fusion, s32[512,512]{1,0:T(8,128)S(1)} %get-tuple-element.7, f32[2,512]{1,0:T(2,128)S(1)} %bitcast.75, ...), kind=kOutput, calls=%fused_computation.8 | convolution fusion | flops 540278784 | bytes 4726794 | tf_op jit(solution)/shard_map/hts,shd->thd/dot_general | solution.py:58
  125.9 5.8 %multiply_reduce_fusion = f32[2,256,256]{2,1,0:T(8,128)S(1)} fusion(bf16[2,32,256,256]{3,2,0,1:T(8,128)(2,1)} %bitcast.65, f32[2,32]{0,1:T(8,128)S(1)} %select_bitcast_fusion), kind=kLoop, calls=%fused_computation | loop fusion | flops 12451840 | bytes 8913152 | tf_op jit(solution)/shard_map/nh,nhde->hde/dot_general | solution.py:88
  131.8 1.1 fusion.47
  133.2 0.3 copy.44
  133.5 0.6 copy-done.3
  134.1 6.6 %convolution_convert_fusion = bf16[512,4096]{1,0:T(8,128)(2,1)} fusion(bf16[512,4096]{1,0:T(8,128)(2,1)} %param.15, bf16[512,512]{1,0:T(8,128)(2,1)S(1)} %copy-done.3, f32[512,512]{1,0:T(8,128)S(1)} %copy.44, f32[512]{0:T(512)S(1)} %convert_element_type.60), kind=kOutput, calls=%fused_computation.1 | convolution fusion | flops 2151677952 | bytes 9963520 | tf_op jit(solution)/shard_map/dot_general | solution.py:105
  140.7 44.3 %reduce-scatter.2.cloned.1.call-done = bf16[64,4096]{1,0:T(8,128)(2,1)} async-done(((bf16[512,4096]{1,0:T(8,128)(2,1)}), bf16[64,4096]{1,0:T(8,128)(2,1)}) %reduce-scatter.2.cloned.1.call-update) | async-done | bytes 524304 | tf_op jit(solution)/shard_map/reduce_scatter | solution.py:104
  (46 shorter events, 1.7 us)
Async XLA Ops:
  6.5 16.7 %copy-start.5 = (u32[256]{0:T(256)S(1)}, u32[256]{0:T(256)}, u32[]{:S(2)}) copy-start(u32[256]{0:T(256)} %constant.78) | copy-start | bytes 3076
  6.5 6.5 %copy-start.1 = (bf16[2,512]{1,0:T(2,128)(2,1)S(1)}, bf16[2,512]{1,0:T(2,128)(2,1)}, u32[]{:S(2)}) copy-start(bf16[2,512]{1,0:T(2,128)(2,1)} %param.12) | copy-start | bytes 6148
  6.5 110.4 %copy-start.4 = (s32[2]{0:T(128)S(1)}, s32[2]{0:T(128)}, u32[]{:S(2)}) copy-start(s32[2]{0:T(128)} %param.13) | copy-start | bytes 28
  6.5 119.3 %all-gather.4.cloned.1.call-start = ((), (), s32[]{:S(2)}) async-start(), calls=%async_computation.2 | async-start | bytes 8650752 | tf_op jit(solution)/shard_map/all_gather | solution.py:75
  12.9 172.0 %reduce-scatter.2.cloned.1.call-start = ((), (), s32[]{:S(2)}) async-start(), calls=%async_computation.1 | async-start | bytes 4718592 | tf_op jit(solution)/shard_map/reduce_scatter | solution.py:104
  13.0 107.8 %collective-permute-start.1 = (bf16[2,512]{1,0:T(2,128)(2,1)S(1)}, bf16[2,512]{1,0:T(2,128)(2,1)S(1)}, u32[]{:S(2)}, u32[]{:S(2)}) collective-permute-start(bf16[2,512]{1,0:T(2,128)(2,1)S(1)} %copy-done.1), channel_id=1, source_target_pairs={{0,8},{8,16},{16,24},{24,32},{32,40},{40,48},{48,56},{56,64},{64,7... | collective-permute-start | bytes 6152 | tf_op jit(solution)/shard_map/ppermute | solution.py:15
  16.5 106.5 %collective-permute-start = (bf16[512,512]{0,1:T(8,128)(2,1)S(1)}, bf16[512,512]{0,1:T(8,128)(2,1)}, u32[]{:S(2)}, u32[]{:S(2)}) collective-permute-start(bf16[512,512]{0,1:T(8,128)(2,1)S(1)} %copy.56), channel_id=1, source_target_pairs={{0,8},{8,16},{16,24},{24,32},{32,40},{40,48},{48,56},{56,64},{64,7... | collective-permute-start | bytes 1572872 | tf_op jit(solution)/shard_map/ppermute | solution.py:15
  19.7 102.3 %collective-permute-start.2 = (bf16[512,512]{1,0:T(8,128)(2,1)}, bf16[512,512]{1,0:T(8,128)(2,1)S(1)}, u32[]{:S(2)}, u32[]{:S(2)}) collective-permute-start(bf16[512,512]{1,0:T(8,128)(2,1)} %param.10), channel_id=1, source_target_pairs={{0,8},{8,16},{16,24},{24,32},{32,40},{40,48},{48,56},{56,64},{64,7... | collective-permute-start | bytes 1572872 | tf_op jit(solution)/shard_map/ppermute | solution.py:15
  117.2 3.5 %copy-start.2 = (bf16[512]{0:T(512)(128)(2,1)S(1)}, bf16[512]{0:T(512)(128)(2,1)}, u32[]{:S(2)}) copy-start(bf16[512]{0:T(512)(128)(2,1)} %param.14) | copy-start | bytes 3076
  125.9 5.9 %copy-start = (bf16[512,512]{1,0:T(8,128)(2,1)S(1)}, bf16[512,512]{1,0:T(8,128)(2,1)}, u32[]{:S(2)}) copy-start(bf16[512,512]{1,0:T(8,128)(2,1)} %param.8) | copy-start | bytes 1572868
  133.0 1.0 copy-start.3
Sparse Core Ops, SparseCore 0:
  13.1 101.2 all-gather.3
  140.8 44.1 reduce-scatter.1
where the time goes:
time: 192 us
  blocking collectives  91.9 us (48%)
  waiting for transfers between devices  44.3 us (23%)
  matrix products  16.4 us (9%)
  between operations  14.3 us (7%)
  starting transfers between devices  10.2 us (5%)
  other arithmetic  9.25 us (5%)
  local copies, waits for them, and re-layouts  5.37 us (3%)
    unnamed x1, blocking collectives  91.9 us
    reduce_scatter x1, waiting for transfers between devices, on_device(): lax.psum_scatter(jnp.dot(hidden, w_out, preferred_element_type=jnp.float3...  44.3 us
    ppermute x3, starting transfers between devices, from_behind(): lax.ppermute(value, axis, [(source, source + steps) for source in range(i...  10.2 us
    dot_general x1, matrix products, on_device(): jnp.dot(hidden, w_out, preferred_element_type=jnp.float32)  6.56 us
    dot_general x1, other arithmetic, on_device(): jnp.einsum('nh,nhde->hde', factor, states, precision=lax.Precision.HIGHEST)  5.84 us
  transfers between devices with their start and end apart: 5, of which 1 were waited for; matrix products, arithmetic and copies ran while one was open for 5% of the time, Pallas kernels for 0%

commit v1 on v0

v1 whole, which is shorter than its diff:
```python
import functools

import jax
import jax.numpy as jnp
from jax import lax
from jax.experimental import pallas as pl
from jax.experimental.pallas import tpu as pltpu
from jax.sharding import PartitionSpec as P

MESH = pl.DeviceIdType.MESH
F32 = jnp.float32
BF16 = jnp.bfloat16
BLOCK = 256
DH = 256
CHUNK = 512
HALF = CHUNK // 2
PIECE = 64
RING = 4


def nt(a, b):
    return lax.dot_general(a, b, (((1,), (1,)), ((), ())), preferred_element_type=F32)


def tn(a, b):
    return lax.dot_general(a, b, (((0,), (0,)), ((), ())), preferred_element_type=F32)


def nn(a, b):
    return jnp.dot(a, b, preferred_element_type=F32)


def twice(a):
    return jnp.concatenate([a, a], axis=1)


def kernel(
    nseq, nchunk, steps,
    q_hbm, k_hbm, v_hbm, g_hbm, ld_hbm, trunc, gain_hbm, w_hbm,
    out_hbm,
    q, k, v, g, ld, gain, w, w_sib,
    state, first, last, last_in, dec, dec_in, pieces, prefixes, prior,
    ret, gated, grow, hid, mine, theirs, part, passed, direct, summed, out,
    load_sem, dec_sem, one_sem, two_sem, last_sem, wsib_sem, hid_sem, p_send, p_recv, out_sem,
):
    seq, head = lax.axis_index("seq"), lax.axis_index("head")
    x, core = lax.div(head, 2), lax.rem(head, 2)
    right = (seq, lax.rem(x + 1, RING) * 2 + core)
    left = (seq, lax.rem(x + RING - 1, RING) * 2 + core)
    sibling = (seq, x * 2 + 1 - core)
    ahead = (lax.rem(seq + 1, nseq), head)

    barrier = pltpu.get_barrier_semaphore()

    def greet(i, carry):
        pl.semaphore_signal(barrier, inc=1, device_id=(lax.rem(seq + i, nseq), head), device_id_type=MESH)
        return carry

    lax.fori_loop(1, nseq, greet, 0)
    for other in (right, left, sibling):
        pl.semaphore_signal(barrier, inc=1, device_id=other, device_id_type=MESH)

    loads = [
        pltpu.make_async_copy(src, dst, load_sem.at[i])
        for i, (src, dst) in enumerate(
            ((ld_hbm, ld), (k_hbm, k), (v_hbm, v), (q_hbm, q), (g_hbm, g), (gain_hbm, gain), (w_hbm, w))
        )
    ]
    for copy in loads:
        copy.start()

    fast = [trunc[h] < steps for h in range(2)]
    slow_f = [jnp.where(f, 0.0, 1.0).astype(F32) for f in fast]
    lower_i = lax.broadcasted_iota(jnp.int32, (BLOCK, BLOCK), 0)
    lower_j = lax.broadcasted_iota(jnp.int32, (BLOCK, BLOCK), 1)
    causal = lower_j <= lower_i
    tri = jnp.where(causal, 1.0, 0.0).astype(BF16)

    loads[0].wait()
    rates = ld[...].astype(F32)
    down, along, total = {}, {}, {}
    for h in range(2):
        for b in range(2):
            row = jnp.broadcast_to(rates[h : h + 1, b * BLOCK : (b + 1) * BLOCK], (128, BLOCK)).astype(BF16)
            down[h, b] = nt(tri, row)
            along[h, b] = nt(row[:16], tri)[:1]
            total[h, b] = down[h, b][BLOCK - 1 :]
            grow[h, b] = jnp.exp(down[h, b])

    loads[1].wait()
    loads[2].wait()
    for h in range(2):
        cols = pl.ds(h * DH, DH)
        own = []
        for b in range(2):
            rows = pl.ds(b * BLOCK, BLOCK)
            fade = twice(jnp.exp(total[h, b] - down[h, b]))
            own.append(tn((k[rows, cols].astype(F32) * fade).astype(BF16), v[rows, cols]))
        whole = own[0] * twice(jnp.exp(total[h, 1])) + own[1]
        state[pl.ds(h * 16, 16)] = whole.astype(BF16).reshape(16, 16, DH)
        first[h] = own[0]
        last[h] = own[1].astype(BF16)
        dec[h] = jnp.exp(total[h, 0] + total[h, 1]) * slow_f[h]

    pl.semaphore_wait(barrier, nseq + 2)

    def send_one(i, carry):
        t = lax.rem(seq + i, nseq)
        pltpu.make_async_remote_copy(
            state.at[t], pieces.at[seq], one_sem.at[0], one_sem.at[1], device_id=(t, head), device_id_type=MESH
        ).start()
        return carry

    lax.fori_loop(1, nseq, send_one, 0)

    def send_dec(i, carry):
        t = lax.rem(seq + i, nseq)
        pltpu.make_async_remote_copy(
            dec.at[lax.div(t, nseq // 2)], dec_in.at[seq], dec_sem.at[0], dec_sem.at[1],
            device_id=(t, head), device_id_type=MESH,
        ).start()
        return carry

    lax.fori_loop(1, nseq, send_dec, 0)
    pltpu.make_async_copy(state.at[seq], pieces.at[seq], one_sem.at[1]).start()
    pltpu.make_async_copy(dec.at[lax.div(seq, nseq // 2)], dec_in.at[seq], dec_sem.at[1]).start()
    last_copy = pltpu.make_async_remote_copy(
        last, last_in, last_sem.at[0], last_sem.at[1], device_id=ahead, device_id_type=MESH
    )
    last_copy.start()
    w_copy = pltpu.make_async_remote_copy(
        w_hbm, w_sib, wsib_sem.at[0], wsib_sem.at[1], device_id=sibling, device_id_type=MESH
    )
    w_copy.start()

    loads[3].wait()
    for h in range(2):
        cols = pl.ds(h * DH, DH)
        for b in range(2):
            rows = pl.ds(b * BLOCK, BLOCK)
            decay = jnp.exp(jnp.minimum(twice(down[h, b]) - along[h, b], 0.0))
            weights = jnp.where(causal, nt(q[rows, cols], k[rows, cols]) * decay, 0.0).astype(BF16)
            ret[rows, cols] = nn(weights, v[rows, cols])

    def wait_all(buffer, sem):
        pltpu.make_async_copy(buffer, buffer, sem).wait()

    def wait_sent(buffer, sem):
        most = buffer.at[pl.ds(0, nseq - 1)]
        pltpu.make_async_copy(most, most, sem).wait()

    wait_all(dec_in, dec_sem.at[1])
    wait_all(pieces, one_sem.at[1])

    def advance(n, total_state):
        prefixes[n] = total_state.astype(BF16)
        return total_state * twice(dec_in[n]) + pieces[n].astype(F32)

    lax.fori_loop(0, nseq, advance, jnp.zeros((16, DH), F32), unroll=4)

    def send_two(i, carry):
        t = lax.rem(seq + i, nseq)
        pltpu.make_async_remote_copy(
            prefixes.at[t], prior.at[seq], two_sem.at[0], two_sem.at[1], device_id=(t, head), device_id_type=MESH
        ).start()
        return carry

    lax.fori_loop(1, nseq, send_two, 0)
    pltpu.make_async_copy(prefixes.at[seq], prior.at[seq], two_sem.at[1]).start()

    loads[4].wait()
    loads[5].wait()
    gate = g[...].astype(F32)
    gated[...] = gain[...].astype(F32) * (gate / (1.0 + jnp.exp(-gate)))
    wait_sent(state, one_sem.at[0])
    wait_sent(dec_in, dec_sem.at[0])
    last_copy.wait()
    loads[6].wait()

    wait_all(prior, two_sem.at[1])
    started = jnp.where(seq > 0, 1.0, 0.0).astype(F32)
    before = {}
    for h in range(2):
        a = prior[pl.ds(h * 16, 16)].reshape(DH, DH)
        near_state = last_in[h].astype(F32) * ((1.0 - slow_f[h]) * started) + a.astype(F32) * slow_f[h]
        before[h, 0] = a
        before[h, 1] = (near_state * twice(jnp.exp(total[h, 0])) + first[h]).astype(BF16)
    for b in range(2):
        rows = pl.ds(b * BLOCK, BLOCK)
        for h in range(2):
            cols = pl.ds(h * DH, DH)
            kept = ret[rows, cols] + nn(q[rows, cols], before[h, b]) * twice(grow[h, b])
            mean = jnp.mean(kept, axis=1, keepdims=True)
            centered = kept - mean
            var = jnp.mean(centered * centered, axis=1, keepdims=True)
            hid[rows, cols] = (centered * lax.rsqrt(var + 1e-5) * gated[rows, cols]).astype(BF16)

    def rows_of(r, c):
        return pl.ds(pl.multiple_of((lax.rem(x + r, RING) * 2 + c) * PIECE, PIECE), PIECE)

    swaps = []
    for r in range(RING):
        copy = pltpu.make_async_remote_copy(
            hid.at[rows_of(r, 1 - core)], theirs.at[pl.ds(r * PIECE, PIECE)], hid_sem.at[0, r], hid_sem.at[1, r],
            device_id=sibling, device_id_type=MESH,
        )
        copy.start()
        swaps.append(copy)
    for r in range(RING):
        mine[pl.ds(r * PIECE, PIECE)] = hid[rows_of(r, core)]
    w_copy.wait_recv()
    for copy in swaps:
        copy.wait_recv()

    def push(kind, j, side, src, dst, to):
        return pltpu.make_async_remote_copy(
            src, dst, p_send.at[kind, j, side], p_recv.at[kind, j, side], device_id=to, device_id_type=MESH
        )

    def far(j, side):
        return push(0, j, side, part.at[j, 2, side], passed.at[j, side], (left, right)[side])

    def near(j, side):
        return push(1, j, side, part.at[j, (1, 3)[side], side], direct.at[j, side], (right, left)[side])

    def onward(j, side):
        return push(2, j, side, part.at[j, (3, 1)[side], side], summed.at[j, side], (left, right)[side])

    def project(j, carry):
        cols = pl.ds(pl.multiple_of(j * CHUNK, CHUNK), CHUNK)
        product = (nn(mine[...], w[:, cols]) + nn(theirs[...], w_sib[:, cols])).astype(BF16)
        for r in range(RING):
            for side in range(2):
                part[j, r, side] = product[r * PIECE : (r + 1) * PIECE, side * HALF : (side + 1) * HALF]
        far(j, 0).start()
        far(j, 1).start()
        near(j, 0).start()
        near(j, 1).start()
        return carry

    lax.fori_loop(0, nchunk, project, 0)

    def forward(j, carry):
        for side in range(2):
            far(j, side).wait_recv()
            slot = (3, 1)[side]
            part[j, slot, side] = (part[j, slot, side].astype(F32) + passed[j, side].astype(F32)).astype(BF16)
            onward(j, side).start()
        return carry

    lax.fori_loop(0, nchunk, forward, 0)

    def write(j):
        cols = pl.ds(pl.multiple_of(j * CHUNK, CHUNK), CHUNK)
        return pltpu.make_async_copy(out.at[:, cols], out_hbm.at[:, cols], out_sem.at[j])

    def finish(j, carry):
        for side in range(2):
            near(j, side).wait_recv()
            onward(j, side).wait_recv()
            cols = pl.ds(pl.multiple_of(j * CHUNK + side * HALF, HALF), HALF)
            out[:, cols] = (
                part[j, 0, side].astype(F32) + direct[j, side].astype(F32) + summed[j, side].astype(F32)
            ).astype(BF16)
        write(j).start()
        return carry

    lax.fori_loop(0, nchunk, finish, 0)

    def drain(j, carry):
        for side in range(2):
            far(j, side).wait_send()
            near(j, side).wait_send()
            onward(j, side).wait_send()
        write(j).wait()
        return carry

    lax.fori_loop(0, nchunk, drain, 0)
    w_copy.wait_send()
    for copy in swaps:
        copy.wait_send()
    wait_sent(prefixes, two_sem.at[0])


def on_device(queries, keys, values, gate, log_decay, trunc_blocks, norm_gain, w_out):
    nseq = lax.axis_size("seq")
    tokens, width = queries.shape
    columns = w_out.shape[1]
    nchunk = columns // CHUNK
    any_spec = pl.BlockSpec(memory_space=pl.ANY)
    vmem, dma = pltpu.VMEM, pltpu.SemaphoreType.DMA
    return pl.pallas_call(
        functools.partial(kernel, nseq, nchunk, tokens // BLOCK * nseq),
        out_shape=jax.ShapeDtypeStruct((PIECE, columns), BF16),
        in_specs=[any_spec] * 5 + [pl.BlockSpec(memory_space=pltpu.SMEM)] + [any_spec] * 2,
        out_specs=any_spec,
        scratch_shapes=[
            vmem((tokens, width), BF16),
            vmem((tokens, width), BF16),
            vmem((tokens, width), BF16),
            vmem((tokens, width), BF16),
            vmem((2, tokens), BF16),
            vmem((1, width), BF16),
            vmem((width, columns), BF16),
            vmem((width, columns), BF16),
            vmem((nseq, 16, DH), BF16),
            vmem((2, DH, DH), F32),
            vmem((2, DH, DH), BF16),
            vmem((2, DH, DH), BF16),
            vmem((2, 1, 128), F32),
            vmem((nseq, 1, 128), F32),
            vmem((nseq, 16, DH), BF16),
            vmem((nseq, 16, DH), BF16),
            vmem((nseq, 16, DH), BF16),
            vmem((tokens, width), F32),
            vmem((tokens, width), F32),
            vmem((2, 2, BLOCK, 128), F32),
            vmem((tokens, width), BF16),
            vmem((RING * PIECE, width), BF16),
            vmem((RING * PIECE, width), BF16),
            vmem((nchunk, RING, 2, PIECE, HALF), BF16),
            vmem((nchunk, 2, PIECE, HALF), BF16),
            vmem((nchunk, 2, PIECE, HALF), BF16),
            vmem((nchunk, 2, PIECE, HALF), BF16),
            vmem((PIECE, columns), BF16),
            dma((7,)),
            dma((2,)),
            dma((2,)),
            dma((2,)),
            dma((2,)),
            dma((2,)),
            dma((2, RING)),
            dma((3, nchunk, 2)),
            dma((3, nchunk, 2)),
            dma((nchunk,)),
        ],
        compiler_params=pltpu.CompilerParams(
            collective_id=0, has_side_effects=True, vmem_limit_bytes=56 * 2**20
        ),
        cost_estimate=pl.CostEstimate(flops=3 * 10**9, bytes_accessed=7 * 2**20, transcendentals=2**20),
    )(queries, keys, values, gate, log_decay, trunc_blocks, norm_gain.reshape(1, width), w_out)


def solution(mesh):
    in_specs = (
        P("seq", "head"),
        P("seq", "head"),
        P("seq", "head"),
        P("seq", "head"),
        P("head", "seq"),
        P("head"),
        P("head"),
        P("head", None),
    )
    out_specs = P(("seq", "head"), None)
    return jax.shard_map(on_device, mesh=mesh, in_specs=in_specs, out_specs=out_specs, check_vma=False)
```

time: 192 us -> 57.7 us (0.30)
  the two profiles are of different devices: /device:TPU:8 before, /device:TPU:1 now
where the time goes in v1:
time: 57.7 us; the launch traced here: 57.5 us
  Pallas kernels  54.4 us (94%)
  local copies, waits for them, and re-layouts  3.13 us (5%)
    pallas_call x1, Pallas kernels, on_device(): pl.pallas_call(functools.partial(kernel, nseq, nchunk, tokens // BLOCK *...  54.4 us
    unnamed x1, local copies, waits for them, and re-layouts  1.87 us
    reshape x1, local copies, waits for them, and re-layouts, on_device(): norm_gain.reshape(1, width)  1.26 us

profile of v1, /device:TPU:1, one launch (start us, length us, event | category | flops | bytes accessed | tf_op | source)
XLA Modules:
  0.0 57.5 jit_solution(10287345993705249291)
XLA Ops:
  0.0 1.3 %reshape.3.gain_hbm = bf16[1,512]{1,0:T(2,128)(2,1)} reshape(bf16[512]{0:T(512)(128)(2,1)} %param.14) | data formatting | bytes 2048 | tf_op jit(solution)/shard_map/reshape | solution.py:341
  1.3 54.4 %shard_map.82 = bf16[64,4096]{1,0:T(8,128)(2,1)} custom-call(bf16[512,512]{1,0:T(8,128)(2,1)} %q_hbm.1, bf16[512,512]{1,0:T(8,128)(2,1)} %k_hbm.1, bf16[512,512]{1,0:T(8,128)(2,1)} %v_hbm.1, bf16[512,512]{1,0:T(8,128)(2,1)} %g_hbm.1, bf16[2,512]{1,0:T(2,128)(2,1)} %ld_hbm.1, s32[2]{0:T(128)} %trunc.1, bf16[1,512]{1,0:T(2,128)(2,1)} %reshape.3.gain_hbm, ...), custom_call_target="tpu_custom_call" | custom-call | flops 3000000000 | bytes 7340032 | tf_op jit(solution)/shard_map/pallas_call | solution.py:292
  55.7 1.9 %copy.10 = bf16[64,4096]{1,0:T(8,128)(2,1)} copy(bf16[64,4096]{1,0:T(8,128)(2,1)} %shard_map.82) | data formatting | bytes 1048576

commit v2 on v1

--- a/solution.py
+++ b/solution.py
@@ -16,6 +16,8 @@
 HALF = CHUNK // 2
 PIECE = 64
 RING = 4
+GROUP = 8
+SHARE = 2 * DH // GROUP
 
 
 def nt(a, b):
@@ -39,24 +41,45 @@
     q_hbm, k_hbm, v_hbm, g_hbm, ld_hbm, trunc, gain_hbm, w_hbm,
     out_hbm,
     q, k, v, g, ld, gain, w, w_sib,
-    state, first, last, last_in, dec, dec_in, pieces, prefixes, prior,
+    state, first, last, last_in, dec, dec_in, pieces, prefixes, prior, sums, sums_in, fades, fades_in,
     ret, gated, grow, hid, mine, theirs, part, passed, direct, summed, out,
-    load_sem, dec_sem, one_sem, two_sem, last_sem, wsib_sem, hid_sem, p_send, p_recv, out_sem,
+    load_sem, dec_sem, one_sem, two_sem, last_sem, sum_send, sum_recv, fade_send, fade_recv, ready, ready_last,
+    wsib_sem, hid_sem, p_send, p_recv, out_sem,
 ):
     seq, head = lax.axis_index("seq"), lax.axis_index("head")
     x, core = lax.div(head, 2), lax.rem(head, 2)
     right = (seq, lax.rem(x + 1, RING) * 2 + core)
     left = (seq, lax.rem(x + RING - 1, RING) * 2 + core)
     sibling = (seq, x * 2 + 1 - core)
-    ahead = (lax.rem(seq + 1, nseq), head)
+    group, place = lax.div(seq, GROUP), lax.rem(seq, GROUP)
+    groups = nseq // GROUP
+    inside = place < GROUP - 1
+    crossing = jnp.logical_and(place == GROUP - 1, group < groups - 1)
+    crossed = jnp.logical_and(place == 0, group > 0)
+
+    def fellow(i):
+        return group * GROUP + lax.rem(place + i, GROUP)
+
+    def abreast(other):
+        return (other * GROUP + place, head)
 
     barrier = pltpu.get_barrier_semaphore()
 
     def greet(i, carry):
-        pl.semaphore_signal(barrier, inc=1, device_id=(lax.rem(seq + i, nseq), head), device_id_type=MESH)
-        return carry
-
-    lax.fori_loop(1, nseq, greet, 0)
+        pl.semaphore_signal(barrier, inc=1, device_id=(fellow(i), head), device_id_type=MESH)
+        return carry
+
+    def greet_later(other, carry):
+        pl.semaphore_signal(barrier, inc=1, device_id=abreast(other), device_id_type=MESH)
+        return carry
+
+    lax.fori_loop(1, GROUP, greet, 0)
+    lax.fori_loop(group + 1, groups, greet_later, 0)
+
+    @pl.when(crossing)
+    def _():
+        pl.semaphore_signal(barrier, inc=1, device_id=(seq + 1, head), device_id_type=MESH)
+
     for other in (right, left, sibling):
         pl.semaphore_signal(barrier, inc=1, device_id=other, device_id_type=MESH)
 
@@ -97,37 +120,53 @@
             fade = twice(jnp.exp(total[h, b] - down[h, b]))
             own.append(tn((k[rows, cols].astype(F32) * fade).astype(BF16), v[rows, cols]))
         whole = own[0] * twice(jnp.exp(total[h, 1])) + own[1]
-        state[pl.ds(h * 16, 16)] = whole.astype(BF16).reshape(16, 16, DH)
+        state[pl.ds(h * (GROUP // 2), GROUP // 2)] = whole.astype(BF16).reshape(GROUP // 2, SHARE, DH)
         first[h] = own[0]
         last[h] = own[1].astype(BF16)
         dec[h] = jnp.exp(total[h, 0] + total[h, 1]) * slow_f[h]
 
-    pl.semaphore_wait(barrier, nseq + 2)
+    pl.semaphore_wait(barrier, GROUP + 2 + group + jnp.where(crossed, 1, 0))
+
+    def tell(other, carry):
+        pl.semaphore_signal(ready.at[group], inc=1, device_id=abreast(other), device_id_type=MESH)
+        return carry
+
+    lax.fori_loop(0, group, tell, 0)
+
+    @pl.when(crossed)
+    def _():
+        pl.semaphore_signal(ready_last, inc=1, device_id=(seq - 1, head), device_id_type=MESH)
 
     def send_one(i, carry):
-        t = lax.rem(seq + i, nseq)
+        t = lax.rem(place + i, GROUP)
         pltpu.make_async_remote_copy(
-            state.at[t], pieces.at[seq], one_sem.at[0], one_sem.at[1], device_id=(t, head), device_id_type=MESH
+            state.at[t], pieces.at[place], one_sem.at[0], one_sem.at[1],
+            device_id=(fellow(i), head), device_id_type=MESH,
         ).start()
         return carry
 
-    lax.fori_loop(1, nseq, send_one, 0)
+    lax.fori_loop(1, GROUP, send_one, 0)
 
     def send_dec(i, carry):
-        t = lax.rem(seq + i, nseq)
+        t = lax.rem(place + i, GROUP)
         pltpu.make_async_remote_copy(
-            dec.at[lax.div(t, nseq // 2)], dec_in.at[seq], dec_sem.at[0], dec_sem.at[1],
-            device_id=(t, head), device_id_type=MESH,
+            dec.at[lax.div(t, GROUP // 2)], dec_in.at[place], dec_sem.at[0], dec_sem.at[1],
+            device_id=(fellow(i), head), device_id_type=MESH,
         ).start()
         return carry
 
-    lax.fori_loop(1, nseq, send_dec, 0)
-    pltpu.make_async_copy(state.at[seq], pieces.at[seq], one_sem.at[1]).start()
-    pltpu.make_async_copy(dec.at[lax.div(seq, nseq // 2)], dec_in.at[seq], dec_sem.at[1]).start()
+    lax.fori_loop(1, GROUP, send_dec, 0)
+    pltpu.make_async_copy(state.at[place], pieces.at[place], one_sem.at[1]).start()
+    pltpu.make_async_copy(dec.at[lax.div(place, GROUP // 2)], dec_in.at[place], dec_sem.at[1]).start()
+
     last_copy = pltpu.make_async_remote_copy(
-        last, last_in, last_sem.at[0], last_sem.at[1], device_id=ahead, device_id_type=MESH
+        last, last_in, last_sem.at[0], last_sem.at[1], device_id=(lax.rem(seq + 1, nseq), head), device_id_type=MESH
     )
-    last_copy.start()
+
+    @pl.when(inside)
+    def _():
+        last_copy.start()
+
     w_copy = pltpu.make_async_remote_copy(
         w_hbm, w_sib, wsib_sem.at[0], wsib_sem.at[1], device_id=sibling, device_id_type=MESH
     )
@@ -142,47 +181,103 @@
             weights = jnp.where(causal, nt(q[rows, cols], k[rows, cols]) * decay, 0.0).astype(BF16)
             ret[rows, cols] = nn(weights, v[rows, cols])
 
+    @pl.when(crossing)
+    def _():
+        pl.semaphore_wait(ready_last, 1)
+        last_copy.start()
+
     def wait_all(buffer, sem):
         pltpu.make_async_copy(buffer, buffer, sem).wait()
 
     def wait_sent(buffer, sem):
-        most = buffer.at[pl.ds(0, nseq - 1)]
+        most = buffer.at[pl.ds(0, GROUP - 1)]
         pltpu.make_async_copy(most, most, sem).wait()
 
     wait_all(dec_in, dec_sem.at[1])
     wait_all(pieces, one_sem.at[1])
 
-    def advance(n, total_state):
+    so_far, fade_so_far = jnp.zeros((SHARE, DH), F32), jnp.ones((1, 128), F32)
+    for n in range(GROUP):
+        so_far = so_far * twice(dec_in[n]) + pieces[n].astype(F32)
+        fade_so_far = fade_so_far * dec_in[n]
+    sums[...] = so_far.astype(BF16)
+    fades[...] = fade_so_far
+
+    def sum_copy(source, target):
+        return pltpu.make_async_remote_copy(
+            sums, sums_in.at[source], sum_send.at[target], sum_recv.at[source],
+            device_id=abreast(target), device_id_type=MESH,
+        )
+
+    def fade_copy(source, target):
+        return pltpu.make_async_remote_copy(
+            fades, fades_in.at[source], fade_send.at[target], fade_recv.at[source],
+            device_id=abreast(target), device_id_type=MESH,
+        )
+
+    def send_sum(other, carry):
+        pl.semaphore_wait(ready.at[other], 1)
+        sum_copy(group, other).start()
+        fade_copy(group, other).start()
+        return carry
+
+    lax.fori_loop(group + 1, groups, send_sum, 0)
+
+    def add_group(other, total_state):
+        fade_copy(other, group).wait_recv()
+        sum_copy(other, group).wait_recv()
+        return total_state * twice(fades_in[other]) + sums_in[other].astype(F32)
+
+    total_state = lax.fori_loop(0, group, add_group, jnp.zeros((SHARE, DH), F32))
+
+    for n in range(GROUP):
         prefixes[n] = total_state.astype(BF16)
-        return total_state * twice(dec_in[n]) + pieces[n].astype(F32)
-
-    lax.fori_loop(0, nseq, advance, jnp.zeros((16, DH), F32), unroll=4)
+        total_state = total_state * twice(dec_in[n]) + pieces[n].astype(F32)
 
     def send_two(i, carry):
-        t = lax.rem(seq + i, nseq)
+        t = lax.rem(place + i, GROUP)
         pltpu.make_async_remote_copy(
-            prefixes.at[t], prior.at[seq], two_sem.at[0], two_sem.at[1], device_id=(t, head), device_id_type=MESH
+            prefixes.at[t], prior.at[place], two_sem.at[0], two_sem.at[1],
+            device_id=(fellow(i), head), device_id_type=MESH,
         ).start()
         return carry
 
-    lax.fori_loop(1, nseq, send_two, 0)
-    pltpu.make_async_copy(prefixes.at[seq], prior.at[seq], two_sem.at[1]).start()
+    lax.fori_loop(1, GROUP, send_two, 0)
+    pltpu.make_async_copy(prefixes.at[place], prior.at[place], two_sem.at[1]).start()
 
     loads[4].wait()
     loads[5].wait()
-    gate = g[...].astype(F32)
-    gated[...] = gain[...].astype(F32) * (gate / (1.0 + jnp.exp(-gate)))
+    gate, width = g[...].astype(F32), g.shape[1]
+    gated[...] = gain[...].astype(F32).reshape(1, width) * (gate / (1.0 + jnp.exp(-gate)))
     wait_sent(state, one_sem.at[0])
     wait_sent(dec_in, dec_sem.at[0])
-    last_copy.wait()
+
+    @pl.when(jnp.logical_or(inside, crossing))
+    def _():
+        last_copy.wait_send()
+
+    def sums_sent(other, carry):
+        sum_copy(group, other).wait_send()
+        fade_copy(group, other).wait_send()
+        return carry
+
+    lax.fori_loop(group + 1, groups, sums_sent, 0)
     loads[6].wait()
 
+    @pl.when(seq > 0)
+    def _():
+        last_copy.wait_recv()
+
+    @pl.when(seq == 0)
+    def _():
+        last_in[...] = jnp.zeros_like(last_in)
+
+
     wait_all(prior, two_sem.at[1])
-    started = jnp.where(seq > 0, 1.0, 0.0).astype(F32)
     before = {}
     for h in range(2):
-        a = prior[pl.ds(h * 16, 16)].reshape(DH, DH)
-        near_state = last_in[h].astype(F32) * ((1.0 - slow_f[h]) * started) + a.astype(F32) * slow_f[h]
+        a = prior[pl.ds(h * (GROUP // 2), GROUP // 2)].reshape(DH, DH)
+        near_state = last_in[h].astype(F32) * (1.0 - slow_f[h]) + a.astype(F32) * slow_f[h]
         before[h, 0] = a
         before[h, 1] = (near_state * twice(jnp.exp(total[h, 0])) + first[h]).astype(BF16)
     for b in range(2):
@@ -286,7 +381,7 @@
     nseq = lax.axis_size("seq")
     tokens, width = queries.shape
     columns = w_out.shape[1]
-    nchunk = columns // CHUNK
+    nchunk, groups = columns // CHUNK, nseq // GROUP
     any_spec = pl.BlockSpec(memory_space=pl.ANY)
     vmem, dma = pltpu.VMEM, pltpu.SemaphoreType.DMA
     return pl.pallas_call(
@@ -300,18 +395,22 @@
             vmem((tokens, width), BF16),
             vmem((tokens, width), BF16),
             vmem((2, tokens), BF16),
-            vmem((1, width), BF16),
+            vmem((width,), BF16),
             vmem((width, columns), BF16),
             vmem((width, columns), BF16),
-            vmem((nseq, 16, DH), BF16),
+            vmem((GROUP, SHARE, DH), BF16),
             vmem((2, DH, DH), F32),
             vmem((2, DH, DH), BF16),
             vmem((2, DH, DH), BF16),
             vmem((2, 1, 128), F32),
-            vmem((nseq, 1, 128), F32),
-            vmem((nseq, 16, DH), BF16),
-            vmem((nseq, 16, DH), BF16),
-            vmem((nseq, 16, DH), BF16),
+            vmem((GROUP, 1, 128), F32),
+            vmem((GROUP, SHARE, DH), BF16),
+            vmem((GROUP, SHARE, DH), BF16),
+            vmem((GROUP, SHARE, DH), BF16),
+            vmem((SHARE, DH), BF16),
+            vmem((groups, SHARE, DH), BF16),
+            vmem((1, 128), F32),
+            vmem((groups, 1, 128), F32),
             vmem((tokens, width), F32),
             vmem((tokens, width), F32),
             vmem((2, 2, BLOCK, 128), F32),
@@ -328,6 +427,12 @@
             dma((2,)),
             dma((2,)),
             dma((2,)),
+            dma((groups,)),
+            dma((groups,)),
+            dma((groups,)),
+            dma((groups,)),
+            pltpu.SemaphoreType.REGULAR((groups,)),
+            pltpu.SemaphoreType.REGULAR,
             dma((2,)),
             dma((2, RING)),
             dma((3, nchunk, 2)),
@@ -338,7 +443,7 @@
             collective_id=0, has_side_effects=True, vmem_limit_bytes=56 * 2**20
         ),
         cost_estimate=pl.CostEstimate(flops=3 * 10**9, bytes_accessed=7 * 2**20, transcendentals=2**20),
-    )(queries, keys, values, gate, log_decay, trunc_blocks, norm_gain.reshape(1, width), w_out)
+    )(queries, keys, values, gate, log_decay, trunc_blocks, norm_gain, w_out)
 
 
 def solution(mesh):

time: 57.7 us -> 48.5 us (0.84)
  the two profiles are of different devices: /device:TPU:1 before, /device:TPU:129 now
where the time goes in v2:
time: 48.5 us; the launch traced here: 47.8 us
  Pallas kernels  46 us (95%)
  local copies, waits for them, and re-layouts  1.87 us (4%)
    pallas_call x1, Pallas kernels, on_device(): pl.pallas_call(functools.partial(kernel, nseq, nchunk, tokens // BLOCK *...  46 us
    unnamed x1, local copies, waits for them, and re-layouts  1.87 us

profile of v2, /device:TPU:129, one launch (start us, length us, event | category | flops | bytes accessed | tf_op | source)
XLA Modules:
  0.0 47.8 jit_solution(8937767797770578459)
XLA Ops:
  0.0 46.0 %shard_map.82 = bf16[64,4096]{1,0:T(8,128)(2,1)} custom-call(bf16[512,512]{1,0:T(8,128)(2,1)} %q_hbm.1, bf16[512,512]{1,0:T(8,128)(2,1)} %k_hbm.1, bf16[512,512]{1,0:T(8,128)(2,1)} %v_hbm.1, bf16[512,512]{1,0:T(8,128)(2,1)} %g_hbm.1, bf16[2,512]{1,0:T(2,128)(2,1)} %ld_hbm.1, s32[2]{0:T(128)} %trunc.1, bf16[512]{0:T(512)(128)(2,1)} %gain_hbm.1, ...), custom_call_target="tpu_custom_call" | custom-call | flops 3000000000 | bytes 7340032 | tf_op jit(solution)/shard_map/pallas_call | solution.py:387
  46.0 1.9 %copy.10 = bf16[64,4096]{1,0:T(8,128)(2,1)} copy(bf16[64,4096]{1,0:T(8,128)(2,1)} %shard_map.82) | data formatting | bytes 1048576

commit v3 on v2

--- a/solution.py
+++ b/solution.py
@@ -39,12 +39,12 @@
 def kernel(
     nseq, nchunk, steps,
     q_hbm, k_hbm, v_hbm, g_hbm, ld_hbm, trunc, gain_hbm, w_hbm,
-    out_hbm,
+    out,
     q, k, v, g, ld, gain, w, w_sib,
     state, first, last, last_in, dec, dec_in, pieces, prefixes, prior, sums, sums_in, fades, fades_in,
-    ret, gated, grow, hid, mine, theirs, part, passed, direct, summed, out,
+    ret, gated, grow, hid, mine, theirs, part, passed, direct, summed,
     load_sem, dec_sem, one_sem, two_sem, last_sem, sum_send, sum_recv, fade_send, fade_recv, ready, ready_last,
-    wsib_sem, hid_sem, p_send, p_recv, out_sem,
+    wsib_sem, hid_sem, p_send, p_recv,
 ):
     seq, head = lax.axis_index("seq"), lax.axis_index("head")
     x, core = lax.div(head, 2), lax.rem(head, 2)
@@ -345,10 +345,6 @@
 
     lax.fori_loop(0, nchunk, forward, 0)
 
-    def write(j):
-        cols = pl.ds(pl.multiple_of(j * CHUNK, CHUNK), CHUNK)
-        return pltpu.make_async_copy(out.at[:, cols], out_hbm.at[:, cols], out_sem.at[j])
-
     def finish(j, carry):
         for side in range(2):
             near(j, side).wait_recv()
@@ -357,7 +353,6 @@
             out[:, cols] = (
                 part[j, 0, side].astype(F32) + direct[j, side].astype(F32) + summed[j, side].astype(F32)
             ).astype(BF16)
-        write(j).start()
         return carry
 
     lax.fori_loop(0, nchunk, finish, 0)
@@ -367,7 +362,6 @@
             far(j, side).wait_send()
             near(j, side).wait_send()
             onward(j, side).wait_send()
-        write(j).wait()
         return carry
 
     lax.fori_loop(0, nchunk, drain, 0)
@@ -386,9 +380,9 @@
     vmem, dma = pltpu.VMEM, pltpu.SemaphoreType.DMA
     return pl.pallas_call(
         functools.partial(kernel, nseq, nchunk, tokens // BLOCK * nseq),
-        out_shape=jax.ShapeDtypeStruct((PIECE, columns), BF16),
+        out_shape=pltpu.VMEM((PIECE, columns), BF16),
         in_specs=[any_spec] * 5 + [pl.BlockSpec(memory_space=pltpu.SMEM)] + [any_spec] * 2,
-        out_specs=any_spec,
+        out_specs=pl.BlockSpec(memory_space=vmem),
         scratch_shapes=[
             vmem((tokens, width), BF16),
             vmem((tokens, width), BF16),
@@ -421,7 +415,6 @@
             vmem((nchunk, 2, PIECE, HALF), BF16),
             vmem((nchunk, 2, PIECE, HALF), BF16),
             vmem((nchunk, 2, PIECE, HALF), BF16),
-            vmem((PIECE, columns), BF16),
             dma((7,)),
             dma((2,)),
             dma((2,)),
@@ -437,7 +430,6 @@
             dma((2, RING)),
             dma((3, nchunk, 2)),
             dma((3, nchunk, 2)),
-            dma((nchunk,)),
         ],
         compiler_params=pltpu.CompilerParams(
             collective_id=0, has_side_effects=True, vmem_limit_bytes=56 * 2**20

time: 48.5 us -> 46.8 us (0.965)
  local copies, waits for them, and re-layouts: 1.87 us -> 0.8 us
  Pallas kernels: 46 us -> 45.3 us
    unnamed x1, local copies, waits for them, and re-layouts: 1.87 us -> 0.8 us
    pallas_call x1, Pallas kernels: 46 us -> 45.3 us  [on_device(): pl.pallas_call(functools.partial(kernel, nseq, nchunk, tokens // BLOCK *...]
where the time goes in v3:
time: 46.8 us; the launch traced here: 46.1 us
  Pallas kernels  45.3 us (97%)
  local copies, waits for them, and re-layouts  0.8 us (2%)
    pallas_call x1, Pallas kernels, on_device(): pl.pallas_call(functools.partial(kernel, nseq, nchunk, tokens // BLOCK *...  45.3 us

profile of v3, /device:TPU:129, one launch (start us, length us, event | category | flops | bytes accessed | tf_op | source)
XLA Modules:
  0.0 46.1 jit_solution(4044426450616388412)
XLA Ops:
  0.0 45.3 %shard_map.82 = bf16[64,4096]{1,0:T(8,128)(2,1)S(1)} custom-call(bf16[512,512]{1,0:T(8,128)(2,1)} %q_hbm.1, bf16[512,512]{1,0:T(8,128)(2,1)} %k_hbm.1, bf16[512,512]{1,0:T(8,128)(2,1)} %v_hbm.1, bf16[512,512]{1,0:T(8,128)(2,1)} %g_hbm.1, bf16[2,512]{1,0:T(2,128)(2,1)} %ld_hbm.1, s32[2]{0:T(128)} %trunc.1, bf16[512]{0:T(512)(128)(2,1)} %gain_hbm.1, ...), custom_call_target="tpu_custom_call" | custom-call | flops 3000000000 | bytes 7340032 | tf_op jit(solution)/shard_map/pallas_call | solution.py:381
  45.3 0.8 %copy.10 = bf16[64,4096]{1,0:T(8,128)(2,1)} copy(bf16[64,4096]{1,0:T(8,128)(2,1)S(1)} %shard_map.82) | data formatting | bytes 1048576

commit v4 on v3

--- a/solution.py
+++ b/solution.py
@@ -159,13 +159,15 @@
     pltpu.make_async_copy(state.at[place], pieces.at[place], one_sem.at[1]).start()
     pltpu.make_async_copy(dec.at[lax.div(place, GROUP // 2)], dec_in.at[place], dec_sem.at[1]).start()
 
-    last_copy = pltpu.make_async_remote_copy(
-        last, last_in, last_sem.at[0], last_sem.at[1], device_id=(lax.rem(seq + 1, nseq), head), device_id_type=MESH
-    )
+    def last_copy(h):
+        return pltpu.make_async_remote_copy(
+            last.at[h], last_in.at[h], last_sem.at[0, h], last_sem.at[1, h],
+            device_id=(lax.rem(seq + 1, nseq), head), device_id_type=MESH,
+        )
 
     @pl.when(inside)
     def _():
-        last_copy.start()
+        last_copy(0).start()
 
     w_copy = pltpu.make_async_remote_copy(
         w_hbm, w_sib, wsib_sem.at[0], wsib_sem.at[1], device_id=sibling, device_id_type=MESH
@@ -184,7 +186,7 @@
     @pl.when(crossing)
     def _():
         pl.semaphore_wait(ready_last, 1)
-        last_copy.start()
+        last_copy(0).start()
 
     def wait_all(buffer, sem):
         pltpu.make_async_copy(buffer, buffer, sem).wait()
@@ -223,6 +225,10 @@
 
     lax.fori_loop(group + 1, groups, send_sum, 0)
 
+    @pl.when(jnp.logical_or(inside, crossing))
+    def _():
+        last_copy(1).start()
+
     def add_group(other, total_state):
         fade_copy(other, group).wait_recv()
         sum_copy(other, group).wait_recv()
@@ -254,7 +260,8 @@
 
     @pl.when(jnp.logical_or(inside, crossing))
     def _():
-        last_copy.wait_send()
+        last_copy(0).wait_send()
+        last_copy(1).wait_send()
 
     def sums_sent(other, carry):
         sum_copy(group, other).wait_send()
@@ -266,7 +273,8 @@
 
     @pl.when(seq > 0)
     def _():
-        last_copy.wait_recv()
+        last_copy(0).wait_recv()
+        last_copy(1).wait_recv()
 
     @pl.when(seq == 0)
     def _():
@@ -419,7 +427,7 @@
             dma((2,)),
             dma((2,)),
             dma((2,)),
-            dma((2,)),
+            dma((2, 2)),
             dma((groups,)),
             dma((groups,)),
             dma((groups,)),

time: 46.8 us -> 45.3 us (0.968); the launches traced: 46.1 us -> 45.2 us
  Pallas kernels: 45.3 us -> 44.4 us
    pallas_call x1, Pallas kernels: 45.3 us -> 44.4 us  [on_device(): pl.pallas_call(functools.partial(kernel, nseq, nchunk, tokens // BLOCK *...]
where the time goes in v4:
time: 45.3 us; the launch traced here: 45.2 us
  Pallas kernels  44.4 us (98%)
  local copies, waits for them, and re-layouts  0.8 us (2%)
    pallas_call x1, Pallas kernels, on_device(): pl.pallas_call(functools.partial(kernel, nseq, nchunk, tokens // BLOCK *...  44.4 us

profile of v4, /device:TPU:129, one launch (start us, length us, event | category | flops | bytes accessed | tf_op | source)
XLA Modules:
  0.0 45.2 jit_solution(6155844058914347285)
XLA Ops:
  0.0 44.4 %shard_map.82 = bf16[64,4096]{1,0:T(8,128)(2,1)S(1)} custom-call(bf16[512,512]{1,0:T(8,128)(2,1)} %q_hbm.1, bf16[512,512]{1,0:T(8,128)(2,1)} %k_hbm.1, bf16[512,512]{1,0:T(8,128)(2,1)} %v_hbm.1, bf16[512,512]{1,0:T(8,128)(2,1)} %g_hbm.1, bf16[2,512]{1,0:T(2,128)(2,1)} %ld_hbm.1, s32[2]{0:T(128)} %trunc.1, bf16[512]{0:T(512)(128)(2,1)} %gain_hbm.1, ...), custom_call_target="tpu_custom_call" | custom-call | flops 3000000000 | bytes 7340032 | tf_op jit(solution)/shard_map/pallas_call | solution.py:389
  44.4 0.8 %copy.10 = bf16[64,4096]{1,0:T(8,128)(2,1)} copy(bf16[64,4096]{1,0:T(8,128)(2,1)S(1)} %shard_map.82) | data formatting | bytes 1048576

commit v5 on v4

--- a/solution.py
+++ b/solution.py
@@ -38,9 +38,9 @@
 
 def kernel(
     nseq, nchunk, steps,
-    q_hbm, k_hbm, v_hbm, g_hbm, ld_hbm, trunc, gain_hbm, w_hbm,
+    q_hbm, k_hbm, v_hbm, g_hbm, ld_hbm, trunc_hbm, gain_hbm, w_hbm,
     out,
-    q, k, v, g, ld, gain, w, w_sib,
+    q, k, v, g, ld, trunc, gain, w, w_sib,
     state, first, last, last_in, dec, dec_in, pieces, prefixes, prior, sums, sums_in, fades, fades_in,
     ret, gated, grow, hid, mine, theirs, part, passed, direct, summed,
     load_sem, dec_sem, one_sem, two_sem, last_sem, sum_send, sum_recv, fade_send, fade_recv, ready, ready_last,
@@ -86,12 +86,13 @@
     loads = [
         pltpu.make_async_copy(src, dst, load_sem.at[i])
         for i, (src, dst) in enumerate(
-            ((ld_hbm, ld), (k_hbm, k), (v_hbm, v), (q_hbm, q), (g_hbm, g), (gain_hbm, gain), (w_hbm, w))
+            ((ld_hbm, ld), (k_hbm, k), (v_hbm, v), (q_hbm, q), (g_hbm, g), (gain_hbm, gain), (w_hbm, w), (trunc_hbm, trunc))
         )
     ]
     for copy in loads:
         copy.start()
 
+    loads[7].wait()
     fast = [trunc[h] < steps for h in range(2)]
     slow_f = [jnp.where(f, 0.0, 1.0).astype(F32) for f in fast]
     lower_i = lax.broadcasted_iota(jnp.int32, (BLOCK, BLOCK), 0)
@@ -389,7 +390,7 @@
     return pl.pallas_call(
         functools.partial(kernel, nseq, nchunk, tokens // BLOCK * nseq),
         out_shape=pltpu.VMEM((PIECE, columns), BF16),
-        in_specs=[any_spec] * 5 + [pl.BlockSpec(memory_space=pltpu.SMEM)] + [any_spec] * 2,
+        in_specs=[any_spec] * 8,
         out_specs=pl.BlockSpec(memory_space=vmem),
         scratch_shapes=[
             vmem((tokens, width), BF16),
@@ -397,6 +398,7 @@
             vmem((tokens, width), BF16),
             vmem((tokens, width), BF16),
             vmem((2, tokens), BF16),
+            pltpu.SMEM((2,), jnp.int32),
             vmem((width,), BF16),
             vmem((width, columns), BF16),
             vmem((width, columns), BF16),
@@ -423,7 +425,7 @@
             vmem((nchunk, 2, PIECE, HALF), BF16),
             vmem((nchunk, 2, PIECE, HALF), BF16),
             vmem((nchunk, 2, PIECE, HALF), BF16),
-            dma((7,)),
+            dma((8,)),
             dma((2,)),
             dma((2,)),
             dma((2,)),

time: 45.3 us -> 44.5 us (0.982)
  Pallas kernels: 44.4 us -> 43.7 us
    pallas_call x1, Pallas kernels: 44.4 us -> 43.7 us  [on_device(): pl.pallas_call(functools.partial(kernel, nseq, nchunk, tokens // BLOCK *...]
where the time goes in v5:
time: 44.5 us
  Pallas kernels  43.7 us (98%)
  local copies, waits for them, and re-layouts  0.8 us (2%)
    pallas_call x1, Pallas kernels, on_device(): pl.pallas_call(functools.partial(kernel, nseq, nchunk, tokens // BLOCK *...  43.7 us

profile of v5, /device:TPU:129, one launch (start us, length us, event | category | flops | bytes accessed | tf_op | source)
XLA Modules:
  0.0 44.5 jit_solution(12139536432740253071)
XLA Ops:
  0.0 43.7 %shard_map.82 = bf16[64,4096]{1,0:T(8,128)(2,1)S(1)} custom-call(bf16[512,512]{1,0:T(8,128)(2,1)} %q_hbm.1, bf16[512,512]{1,0:T(8,128)(2,1)} %k_hbm.1, bf16[512,512]{1,0:T(8,128)(2,1)} %v_hbm.1, bf16[512,512]{1,0:T(8,128)(2,1)} %g_hbm.1, bf16[2,512]{1,0:T(2,128)(2,1)} %ld_hbm.1, s32[2]{0:T(128)} %trunc_hbm.1, bf16[512]{0:T(512)(128)(2,1)} %gain_hbm.1, ...), custom_call_target="tpu_custom_call" | custom-call | flops 3000000000 | bytes 7340032 | tf_op jit(solution)/shard_map/pallas_call | solution.py:390
  43.7 0.8 %copy.10 = bf16[64,4096]{1,0:T(8,128)(2,1)} copy(bf16[64,4096]{1,0:T(8,128)(2,1)S(1)} %shard_map.82) | data formatting | bytes 1048576

commit v6 on v5

--- a/solution.py
+++ b/solution.py
@@ -12,7 +12,7 @@
 BF16 = jnp.bfloat16
 BLOCK = 256
 DH = 256
-CHUNK = 512
+CHUNK = 1024
 HALF = CHUNK // 2
 PIECE = 64
 RING = 4
@@ -42,7 +42,7 @@
     out,
     q, k, v, g, ld, trunc, gain, w, w_sib,
     state, first, last, last_in, dec, dec_in, pieces, prefixes, prior, sums, sums_in, fades, fades_in,
-    ret, gated, grow, hid, mine, theirs, part, passed, direct, summed,
+    ret, gated, grow, hid, mine, theirs, part, passed, direct, summed, own,
     load_sem, dec_sem, one_sem, two_sem, last_sem, sum_send, sum_recv, fade_send, fade_recv, ready, ready_last,
     wsib_sem, hid_sem, p_send, p_recv,
 ):
@@ -115,15 +115,15 @@
     loads[2].wait()
     for h in range(2):
         cols = pl.ds(h * DH, DH)
-        own = []
+        states = []
         for b in range(2):
             rows = pl.ds(b * BLOCK, BLOCK)
             fade = twice(jnp.exp(total[h, b] - down[h, b]))
-            own.append(tn((k[rows, cols].astype(F32) * fade).astype(BF16), v[rows, cols]))
-        whole = own[0] * twice(jnp.exp(total[h, 1])) + own[1]
+            states.append(tn((k[rows, cols].astype(F32) * fade).astype(BF16), v[rows, cols]))
+        whole = states[0] * twice(jnp.exp(total[h, 1])) + states[1]
         state[pl.ds(h * (GROUP // 2), GROUP // 2)] = whole.astype(BF16).reshape(GROUP // 2, SHARE, DH)
-        first[h] = own[0]
-        last[h] = own[1].astype(BF16)
+        first[h] = states[0]
+        last[h] = states[1].astype(BF16)
         dec[h] = jnp.exp(total[h, 0] + total[h, 1]) * slow_f[h]
 
     pl.semaphore_wait(barrier, GROUP + 2 + group + jnp.where(crossed, 1, 0))
@@ -354,30 +354,29 @@
 
     lax.fori_loop(0, nchunk, forward, 0)
 
-    def finish(j, carry):
-        for side in range(2):
-            near(j, side).wait_recv()
-            onward(j, side).wait_recv()
-            cols = pl.ds(pl.multiple_of(j * CHUNK + side * HALF, HALF), HALF)
-            out[:, cols] = (
-                part[j, 0, side].astype(F32) + direct[j, side].astype(F32) + summed[j, side].astype(F32)
-            ).astype(BF16)
-        return carry
-
-    lax.fori_loop(0, nchunk, finish, 0)
-
-    def drain(j, carry):
-        for side in range(2):
-            far(j, side).wait_send()
-            near(j, side).wait_send()
-            onward(j, side).wait_send()
-        return carry
-
-    lax.fori_loop(0, nchunk, drain, 0)
     w_copy.wait_send()
     for copy in swaps:
         copy.wait_send()
     wait_sent(prefixes, two_sem.at[0])
+
+    def gather(j, carry):
+        for side in range(2):
+            far(j, side).wait_send()
+            near(j, side).wait_send()
+            near(j, side).wait_recv()
+            own[j, side] = part[j, 0, side].astype(F32) + direct[j, side].astype(F32)
+        return carry
+
+    def finish(j, carry):
+        for side in range(2):
+            onward(j, side).wait_recv()
+            cols = pl.ds(pl.multiple_of(j * CHUNK + side * HALF, HALF), HALF)
+            out[:, cols] = (own[j, side] + summed[j, side].astype(F32)).astype(BF16)
+            onward(j, side).wait_send()
+        return carry
+
+    lax.fori_loop(0, nchunk, gather, 0)
+    lax.fori_loop(0, nchunk, finish, 0)
 
 
 def on_device(queries, keys, values, gate, log_decay, trunc_blocks, norm_gain, w_out):
@@ -425,6 +424,7 @@
             vmem((nchunk, 2, PIECE, HALF), BF16),
             vmem((nchunk, 2, PIECE, HALF), BF16),
             vmem((nchunk, 2, PIECE, HALF), BF16),
+            vmem((nchunk, 2, PIECE, HALF), F32),
             dma((8,)),
             dma((2,)),
             dma((2,)),

time: 44.5 us -> 44.3 us (level)
  no operation moved by 1% of the time
where the time goes in v6:
time: 44.3 us; the launch traced here: 44.2 us
  Pallas kernels  43.4 us (98%)
  local copies, waits for them, and re-layouts  0.8 us (2%)
    pallas_call x1, Pallas kernels, on_device(): pl.pallas_call(functools.partial(kernel, nseq, nchunk, tokens // BLOCK *...  43.4 us

profile of v6, /device:TPU:129, one launch (start us, length us, event | category | flops | bytes accessed | tf_op | source)
XLA Modules:
  0.0 44.2 jit_solution(16258263948683069625)
XLA Ops:
  0.0 43.4 %shard_map.82 = bf16[64,4096]{1,0:T(8,128)(2,1)S(1)} custom-call(bf16[512,512]{1,0:T(8,128)(2,1)} %q_hbm.1, bf16[512,512]{1,0:T(8,128)(2,1)} %k_hbm.1, bf16[512,512]{1,0:T(8,128)(2,1)} %v_hbm.1, bf16[512,512]{1,0:T(8,128)(2,1)} %g_hbm.1, bf16[2,512]{1,0:T(2,128)(2,1)} %ld_hbm.1, s32[2]{0:T(128)} %trunc_hbm.1, bf16[512]{0:T(512)(128)(2,1)} %gain_hbm.1, ...), custom_call_target="tpu_custom_call" | custom-call | flops 3000000000 | bytes 7340032 | tf_op jit(solution)/shard_map/pallas_call | solution.py:389
  43.4 0.8 %copy.10 = bf16[64,4096]{1,0:T(8,128)(2,1)} copy(bf16[64,4096]{1,0:T(8,128)(2,1)S(1)} %shard_map.82) | data formatting | bytes 1048576

commit v7 on v6

--- a/solution.py
+++ b/solution.py
@@ -272,49 +272,52 @@
     lax.fori_loop(group + 1, groups, sums_sent, 0)
     loads[6].wait()
 
-    @pl.when(seq > 0)
-    def _():
-        last_copy(0).wait_recv()
-        last_copy(1).wait_recv()
-
-    @pl.when(seq == 0)
-    def _():
-        last_in[...] = jnp.zeros_like(last_in)
-
-
     wait_all(prior, two_sem.at[1])
-    before = {}
-    for h in range(2):
-        a = prior[pl.ds(h * (GROUP // 2), GROUP // 2)].reshape(DH, DH)
-        near_state = last_in[h].astype(F32) * (1.0 - slow_f[h]) + a.astype(F32) * slow_f[h]
-        before[h, 0] = a
-        before[h, 1] = (near_state * twice(jnp.exp(total[h, 0])) + first[h]).astype(BF16)
+    def piece(i, c):
+        return pl.ds(pl.multiple_of((2 * i + c) * PIECE, PIECE), PIECE)
+
+    def slot(i):
+        return pl.ds(pl.multiple_of(lax.rem(i - x + RING, RING) * PIECE, PIECE), PIECE)
+
+    def swap(i):
+        return pltpu.make_async_remote_copy(
+            hid.at[piece(i, 1 - core)], theirs.at[slot(i)], hid_sem.at[0, i], hid_sem.at[1, i],
+            device_id=sibling, device_id_type=MESH,
+        )
+
+    per_block = BLOCK // (2 * PIECE)
     for b in range(2):
         rows = pl.ds(b * BLOCK, BLOCK)
+        if b == 1:
+
+            @pl.when(seq > 0)
+            def _():
+                last_copy(0).wait_recv()
+                last_copy(1).wait_recv()
+
+            @pl.when(seq == 0)
+            def _():
+                last_in[...] = jnp.zeros_like(last_in)
+
         for h in range(2):
             cols = pl.ds(h * DH, DH)
-            kept = ret[rows, cols] + nn(q[rows, cols], before[h, b]) * twice(grow[h, b])
+            before = prior[pl.ds(h * (GROUP // 2), GROUP // 2)].reshape(DH, DH)
+            if b == 1:
+                near_state = last_in[h].astype(F32) * (1.0 - slow_f[h]) + before.astype(F32) * slow_f[h]
+                before = (near_state * twice(jnp.exp(total[h, 0])) + first[h]).astype(BF16)
+            kept = ret[rows, cols] + nn(q[rows, cols], before) * twice(grow[h, b])
             mean = jnp.mean(kept, axis=1, keepdims=True)
             centered = kept - mean
             var = jnp.mean(centered * centered, axis=1, keepdims=True)
             hid[rows, cols] = (centered * lax.rsqrt(var + 1e-5) * gated[rows, cols]).astype(BF16)
-
-    def rows_of(r, c):
-        return pl.ds(pl.multiple_of((lax.rem(x + r, RING) * 2 + c) * PIECE, PIECE), PIECE)
-
-    swaps = []
-    for r in range(RING):
-        copy = pltpu.make_async_remote_copy(
-            hid.at[rows_of(r, 1 - core)], theirs.at[pl.ds(r * PIECE, PIECE)], hid_sem.at[0, r], hid_sem.at[1, r],
-            device_id=sibling, device_id_type=MESH,
-        )
-        copy.start()
-        swaps.append(copy)
-    for r in range(RING):
-        mine[pl.ds(r * PIECE, PIECE)] = hid[rows_of(r, core)]
+        for i in range(b * per_block, (b + 1) * per_block):
+            swap(i).start()
+    for i in range(RING):
+        mine[slot(i)] = hid[piece(i, core)]
+    ahead = nn(mine[...], w[:, :CHUNK])
     w_copy.wait_recv()
-    for copy in swaps:
-        copy.wait_recv()
+    for i in range(RING):
+        swap(i).wait_recv()
 
     def push(kind, j, side, src, dst, to):
         return pltpu.make_async_remote_copy(
@@ -330,9 +333,8 @@
     def onward(j, side):
         return push(2, j, side, part.at[j, (3, 1)[side], side], summed.at[j, side], (left, right)[side])
 
-    def project(j, carry):
-        cols = pl.ds(pl.multiple_of(j * CHUNK, CHUNK), CHUNK)
-        product = (nn(mine[...], w[:, cols]) + nn(theirs[...], w_sib[:, cols])).astype(BF16)
+    def send_parts(j, product):
+        product = product.astype(BF16)
         for r in range(RING):
             for side in range(2):
                 part[j, r, side] = product[r * PIECE : (r + 1) * PIECE, side * HALF : (side + 1) * HALF]
@@ -340,9 +342,14 @@
         far(j, 1).start()
         near(j, 0).start()
         near(j, 1).start()
-        return carry
-
-    lax.fori_loop(0, nchunk, project, 0)
+
+    def project(j, carry):
+        cols = pl.ds(pl.multiple_of(j * CHUNK, CHUNK), CHUNK)
+        send_parts(j, nn(mine[...], w[:, cols]) + nn(theirs[...], w_sib[:, cols]))
+        return carry
+
+    send_parts(0, ahead + nn(theirs[...], w_sib[:, :CHUNK]))
+    lax.fori_loop(1, nchunk, project, 0)
 
     def forward(j, carry):
         for side in range(2):
@@ -355,8 +362,8 @@
     lax.fori_loop(0, nchunk, forward, 0)
 
     w_copy.wait_send()
-    for copy in swaps:
-        copy.wait_send()
+    for i in range(RING):
+        swap(i).wait_send()
     wait_sent(prefixes, two_sem.at[0])
 
     def gather(j, carry):

time: 44.3 us -> 44.4 us (level)
  no operation moved by 1% of the time
where the time goes in v7:
time: 44.4 us; the launch traced here: 44.3 us
  Pallas kernels  43.5 us (98%)
  local copies, waits for them, and re-layouts  0.8 us (2%)
    pallas_call x1, Pallas kernels, on_device(): pl.pallas_call(functools.partial(kernel, nseq, nchunk, tokens // BLOCK *...  43.5 us

profile of v7, /device:TPU:129, one launch (start us, length us, event | category | flops | bytes accessed | tf_op | source)
XLA Modules:
  0.0 44.3 jit_solution(709513864199445909)
XLA Ops:
  0.0 43.5 %shard_map.82 = bf16[64,4096]{1,0:T(8,128)(2,1)S(1)} custom-call(bf16[512,512]{1,0:T(8,128)(2,1)} %q_hbm.1, bf16[512,512]{1,0:T(8,128)(2,1)} %k_hbm.1, bf16[512,512]{1,0:T(8,128)(2,1)} %v_hbm.1, bf16[512,512]{1,0:T(8,128)(2,1)} %g_hbm.1, bf16[2,512]{1,0:T(2,128)(2,1)} %ld_hbm.1, s32[2]{0:T(128)} %trunc_hbm.1, bf16[512]{0:T(512)(128)(2,1)} %gain_hbm.1, ...), custom_call_target="tpu_custom_call" | custom-call | flops 3000000000 | bytes 7340032 | tf_op jit(solution)/shard_map/pallas_call | solution.py:396
  43.5 0.8 %copy.10 = bf16[64,4096]{1,0:T(8,128)(2,1)} copy(bf16[64,4096]{1,0:T(8,128)(2,1)S(1)} %shard_map.82) | data formatting | bytes 1048576

commit v8 on v6

--- a/solution.py
+++ b/solution.py
@@ -128,15 +128,15 @@
 
     pl.semaphore_wait(barrier, GROUP + 2 + group + jnp.where(crossed, 1, 0))
 
-    def tell(other, carry):
-        pl.semaphore_signal(ready.at[group], inc=1, device_id=abreast(other), device_id_type=MESH)
-        return carry
-
-    lax.fori_loop(0, group, tell, 0)
-
-    @pl.when(crossed)
-    def _():
-        pl.semaphore_signal(ready_last, inc=1, device_id=(seq - 1, head), device_id_type=MESH)
+    def send_dec(i, carry):
+        t = lax.rem(place + i, GROUP)
+        pltpu.make_async_remote_copy(
+            dec.at[lax.div(t, GROUP // 2)], dec_in.at[place], dec_sem.at[0], dec_sem.at[1],
+            device_id=(fellow(i), head), device_id_type=MESH,
+        ).start()
+        return carry
+
+    lax.fori_loop(1, GROUP, send_dec, 0)
 
     def send_one(i, carry):
         t = lax.rem(place + i, GROUP)
@@ -148,17 +148,18 @@
 
     lax.fori_loop(1, GROUP, send_one, 0)
 
-    def send_dec(i, carry):
-        t = lax.rem(place + i, GROUP)
-        pltpu.make_async_remote_copy(
-            dec.at[lax.div(t, GROUP // 2)], dec_in.at[place], dec_sem.at[0], dec_sem.at[1],
-            device_id=(fellow(i), head), device_id_type=MESH,
-        ).start()
-        return carry
-
-    lax.fori_loop(1, GROUP, send_dec, 0)
     pltpu.make_async_copy(state.at[place], pieces.at[place], one_sem.at[1]).start()
     pltpu.make_async_copy(dec.at[lax.div(place, GROUP // 2)], dec_in.at[place], dec_sem.at[1]).start()
+
+    def tell(other, carry):
+        pl.semaphore_signal(ready.at[group], inc=1, device_id=abreast(other), device_id_type=MESH)
+        return carry
+
+    lax.fori_loop(0, group, tell, 0)
+
+    @pl.when(crossed)
+    def _():
+        pl.semaphore_signal(ready_last, inc=1, device_id=(seq - 1, head), device_id_type=MESH)
 
     def last_copy(h):
         return pltpu.make_async_remote_copy(

time: 44.3 us -> 44.3 us (level)
  no operation moved by 1% of the time
where the time goes in v8:
time: 44.3 us; the launch traced here: 44.2 us
  Pallas kernels  43.4 us (98%)
  local copies, waits for them, and re-layouts  0.8 us (2%)
    pallas_call x1, Pallas kernels, on_device(): pl.pallas_call(functools.partial(kernel, nseq, nchunk, tokens // BLOCK *...  43.4 us

profile of v8, /device:TPU:129, one launch (start us, length us, event | category | flops | bytes accessed | tf_op | source)
XLA Modules:
  0.0 44.2 jit_solution(16311430271280715000)
XLA Ops:
  0.0 43.4 %shard_map.82 = bf16[64,4096]{1,0:T(8,128)(2,1)S(1)} custom-call(bf16[512,512]{1,0:T(8,128)(2,1)} %q_hbm.1, bf16[512,512]{1,0:T(8,128)(2,1)} %k_hbm.1, bf16[512,512]{1,0:T(8,128)(2,1)} %v_hbm.1, bf16[512,512]{1,0:T(8,128)(2,1)} %g_hbm.1, bf16[2,512]{1,0:T(2,128)(2,1)} %ld_hbm.1, s32[2]{0:T(128)} %trunc_hbm.1, bf16[512]{0:T(512)(128)(2,1)} %gain_hbm.1, ...), custom_call_target="tpu_custom_call" | custom-call | flops 3000000000 | bytes 7340032 | tf_op jit(solution)/shard_map/pallas_call | solution.py:390
  43.4 0.8 %copy.10 = bf16[64,4096]{1,0:T(8,128)(2,1)} copy(bf16[64,4096]{1,0:T(8,128)(2,1)S(1)} %shard_map.82) | data formatting | bytes 1048576

commit v9 on v8

--- a/solution.py
+++ b/solution.py
@@ -221,8 +221,8 @@
 
     def send_sum(other, carry):
         pl.semaphore_wait(ready.at[other], 1)
+        fade_copy(group, other).start()
         sum_copy(group, other).start()
-        fade_copy(group, other).start()
         return carry
 
     lax.fori_loop(group + 1, groups, send_sum, 0)

time: 44.3 us -> 44.8 us (1.011)
  Pallas kernels: 43.4 us -> 43.9 us
    pallas_call x1, Pallas kernels: 43.4 us -> 43.9 us  [on_device(): pl.pallas_call(functools.partial(kernel, nseq, nchunk, tokens // BLOCK *...]
where the time goes in v9:
time: 44.8 us; the launch traced here: 44.7 us
  Pallas kernels  43.9 us (98%)
  local copies, waits for them, and re-layouts  0.8 us (2%)
    pallas_call x1, Pallas kernels, on_device(): pl.pallas_call(functools.partial(kernel, nseq, nchunk, tokens // BLOCK *...  43.9 us

profile of v9, /device:TPU:129, one launch (start us, length us, event | category | flops | bytes accessed | tf_op | source)
XLA Modules:
  0.0 44.7 jit_solution(17904698065802602322)
XLA Ops:
  0.0 43.9 %shard_map.82 = bf16[64,4096]{1,0:T(8,128)(2,1)S(1)} custom-call(bf16[512,512]{1,0:T(8,128)(2,1)} %q_hbm.1, bf16[512,512]{1,0:T(8,128)(2,1)} %k_hbm.1, bf16[512,512]{1,0:T(8,128)(2,1)} %v_hbm.1, bf16[512,512]{1,0:T(8,128)(2,1)} %g_hbm.1, bf16[2,512]{1,0:T(2,128)(2,1)} %ld_hbm.1, s32[2]{0:T(128)} %trunc_hbm.1, bf16[512]{0:T(512)(128)(2,1)} %gain_hbm.1, ...), custom_call_target="tpu_custom_call" | custom-call | flops 3000000000 | bytes 7340032 | tf_op jit(solution)/shard_map/pallas_call | solution.py:390
  43.9 0.8 %copy.10 = bf16[64,4096]{1,0:T(8,128)(2,1)} copy(bf16[64,4096]{1,0:T(8,128)(2,1)S(1)} %shard_map.82) | data formatting | bytes 1048576
